TPU v7x, 32 devices: a whole 2x2x4 slice. The times are simulated.
32 devices in a mesh: parts: 2 (over y), member: 4 (over z), tile: 4 (over x, core).
Axes of the slice: x: 2, y: 2, z: 4, core: 2. Of those that a mesh axis runs over, the one named last changes fastest.
Arguments:
- state: float32 [8, 3, 20, 16, 1024], P(('parts', 'member'), None, None, 'tile'), parts along dimension 0, may hold values from -3 to 3
- parent: int32 [8], P('parts'), parts along dimension 0, may hold values from 0 to 3
- depth: float32 [20], replicated, may hold values from 0.1 to 1
- interp: bfloat16 [8, 128, 4096], P(('parts', 'tile')), parts along dimension 0, may hold values from -0.09375 to 0.09375
- obs: float32 [8, 2, 128], P(('parts', 'tile')), parts along dimension 0, may hold values from -6 to 6
- counts: int32 [8], P(('parts', 'tile')), parts along dimension 0, may hold values from 1 to 128, 256 in all
Outputs:
- predicted_states: float32 [8, 3, 20, 16, 1024], P(('parts', 'member'), None, None, 'tile'), parts along dimension 0
- tracker_mismatch: float32 [8], P(('parts', 'member')), parts along dimension 0
There are 2 independent parts, one for each index of `parts`. A program takes and returns all parts, laid end to end along the dimension named above; an argument that names none is the same for every part. Nothing has to cross between parts.
All inputs are finite; a program needn't handle non-finite values. No bound on the sum of `counts` on one device may be relied on, other than what follows from the above.
Results may differ from a plain program's by a relative error of at most 0.00069.
Values sent between devices are 32-bit elements; how exact they have to be, the bound alone decides.
A program may use at most 64 MiB of HBM per device.

v0:
```python
import jax
import jax.numpy as jnp
from jax import lax
from jax.sharding import PartitionSpec as P

STEPS = 4


time_step = 0.3
nudge_gain = 2.0
coriolis = 0.5
viscosity = 0.05
mixing = 0.1


def with_halo(cells, sides, width):
    for axis, dim in sides:
        count = lax.axis_size(axis)
        ends = count - 1
        head = lax.slice_in_dim(cells, 0, width, axis=dim)
        tail = lax.slice_in_dim(cells, cells.shape[dim] - width, cells.shape[dim], axis=dim)
        cells = jnp.concatenate(
            [
                lax.ppermute(tail, axis, [(i, (i + 1) % count) for i in range(ends)]),
                cells,
                lax.ppermute(head, axis, [((i + 1) % count, i) for i in range(ends)]),
            ],
            axis=dim,
        )
    return cells


def shift_cols(field, nudge_quantity):
    return jnp.roll(field, nudge_quantity, axis=2)


def vertical_mix(field):
    padded = jnp.concatenate([field[:1], field, field[-1:]], axis=0)
    return mixing * (padded[2:] + padded[:-2] - 2.0 * field)


def forward_step(extended, depth):
    u_ext, v_ext, h_ext = (extended[0], extended[1], extended[2])

    def eastward_difference(field):
        return (field[:, 2:] - field[:, :-2]) * 0.5

    def diff_y(field):
        return (shift_cols(field, -1) - shift_cols(field, 1)) * 0.5

    def laplace(field):
        inner = field[:, 1:-1]
        return (
            field[:, 2:]
            + field[:, :-2]
            + shift_cols(inner, -1)
            + shift_cols(inner, 1)
            - 4.0 * inner
        )

    u_core = u_ext[:, 1:-1]
    v_core = v_ext[:, 1:-1]
    interior_height = h_ext[:, 1:-1]
    u_next = u_core + time_step * (
        coriolis * v_core
        - eastward_difference(h_ext)
        + viscosity * laplace(u_ext)
        + vertical_mix(u_core)
    )
    v_next = v_core + time_step * (
        -coriolis * u_core
        - diff_y(interior_height)
        + viscosity * laplace(v_ext)
        + vertical_mix(v_core)
    )
    h_next = h_ext[:, 2:-2] - time_step * depth[:, None, None] * (
        eastward_difference(u_next) + diff_y(v_next[:, 1:-1])
    )
    return jnp.stack([u_next[:, 1:-1], v_next[:, 1:-1], h_next])


def observation_residual(fields, coefficient_array, observed, live):
    rows, cols = (fields.shape[2], fields.shape[3])
    surf = fields[0:2, 0].reshape(2, rows * cols).astype(jnp.bfloat16)
    pred = lax.dot_general(
        surf, coefficient_array, (((1,), (1,)), ((), ())), preferred_element_type=jnp.float32
    )
    return live * (observed - pred)


def per_device(state, parent, depth, interp, obs, counts):
    me = lax.axis_index("member")
    mine = parent[me]
    piece = lax.all_gather(state, "member", axis=0, tiled=True)
    members = jnp.arange(piece.shape[0], dtype=jnp.int32)
    selected = (members == mine).reshape(-1, 1, 1, 1, 1)
    fields = jnp.sum(jnp.where(selected, piece, 0.0), axis=0, keepdims=True)[0]
    coefficient_array = interp[0]
    observed = obs[0]
    slots = coefficient_array.shape[0]
    live = (jnp.arange(slots, dtype=jnp.int32) < counts[0]).astype(jnp.float32)[None, :]
    rows, cols = (fields.shape[2], fields.shape[3])
    for step in range(STEPS):
        innov = observation_residual(fields, coefficient_array, observed, live)
        back = jnp.dot(
            innov.astype(jnp.bfloat16), coefficient_array, preferred_element_type=jnp.float32
        )
        fields = fields.at[0:2, 0].add(time_step * nudge_gain * back.reshape(2, rows, cols))
        extended = with_halo(fields, (("tile", 2),), 2)
        fields = forward_step(extended, depth)
    innov = observation_residual(fields, coefficient_array, observed, live)
    total = lax.psum(0.5 * jnp.sum(innov * innov), "tile")
    return (fields[None], total.reshape(1))


def solution(mesh):
    return jax.shard_map(
        per_device,
        mesh=mesh,
        in_specs=(
            P(("parts", "member"), None, None, "tile", None),
            P("parts"),
            P(),
            P(("parts", "tile"), None, None),
            P(("parts", "tile"), None, None),
            P(("parts", "tile")),
        ),
        out_specs=(P(("parts", "member"), None, None, "tile", None), P(("parts", "member"))),
        check_vma=False,
    )
```

profile of v0, /device:TPU:0, one launch (start us, length us, event | category | flops | bytes accessed | tf_op | source)
XLA Modules:
  0.0 188.4 jit_solution(491833850354872844)
XLA Ops:
  7.2 0.7 all-gather.2.cloned.1.call-update
  8.6 1.6 copy.55
  10.2 0.6 dynamic_slice.3
  10.8 0.6 iota_compare_fusion
  11.5 77.3 %all-gather.2.cloned.1.call-done = f32[4,3,20,4,1024]{4,3,2,1,0:T(4,128)} async-done(((f32[1,3,20,4,1024]{4,3,2,1,0:T(4,128)}), f32[4,3,20,4,1024]{4,3,2,1,0:T(4,128)}) %all-gather.2.cloned.1.call-update) | async-done | bytes 3932176 | tf_op jit(solution)/shard_map/all_gather | solution.py:94
  88.8 3.6 %select_reduce_fusion = f32[3,20,4,1024]{3,2,1,0:T(4,128)S(1)} fusion(f32[4,3,20,4,1024]{4,3,2,1,0:T(4,128)} %all-gather.2.cloned.1.call-done, pred[4]{0:T(512)(128)(4,1)S(1)} %iota_compare_fusion), kind=kLoop, calls=%fused_computation | loop fusion | flops 1720320 | bytes 4915204 | tf_op jit(solution)/shard_map/reduce_sum | solution.py:97
  92.5 1.3 fusion.4
  93.8 0.4 fusion.174
  94.2 1.8 collective-permute-start
  96.0 1.3 collective-permute-start.1
  97.4 3.6 %collective-permute-done.1 = f32[3,20,2,1024]{3,2,1,0:T(2,128)S(1)} collective-permute-done((f32[3,20,2,1024]{3,2,1,0:T(2,128)S(1)}, f32[3,20,2,1024]{3,2,1,0:T(2,128)S(1)}, u32[]{:S(2)}, u32[]{:S(2)}) %collective-permute-start.1) | collective-permute-done | bytes 491552 | tf_op jit(solution)/shard_map/ppermute | solution.py:26
  101.0 0.7 pad_maximum_fusion
  101.8 0.6 fusion.208
  102.9 0.8 fusion.111
  104.1 0.6 fusion.122
  104.8 0.5 slice_bitcast_fusion.15
  105.3 1.2 fusion.30
  106.9 0.4 fusion.173
  107.3 8.8 %collective-permute-start.2 = (f32[3,20,2,1024]{3,2,1,0:T(2,128)S(1)}, f32[3,20,2,1024]{3,2,1,0:T(2,128)S(1)}, u32[]{:S(2)}, u32[]{:S(2)}) collective-permute-start(f32[3,20,2,1024]{3,2,1,0:T(2,128)S(1)} %get-tuple-element.72), channel_id=1, source_target_pairs={{0,1},{1,2},{2,3},{4,5},{5,6},{6,7},{8,9},{9,10},{10,11},{12,13},{... | collective-permute-start | bytes 1474568 | tf_op jit(solution)/shard_map/ppermute | solution.py:24
  116.1 1.5 collective-permute-start.3
  117.6 2.3 %collective-permute-done.3 = f32[3,20,2,1024]{3,2,1,0:T(2,128)S(1)} collective-permute-done((f32[3,20,2,1024]{3,2,1,0:T(2,128)S(1)}, f32[3,20,2,1024]{3,2,1,0:T(2,128)S(1)}, u32[]{:S(2)}, u32[]{:S(2)}) %collective-permute-start.3) | collective-permute-done | bytes 491552 | tf_op jit(solution)/shard_map/ppermute | solution.py:26
  119.9 0.6 pad_maximum_fusion.1
  121.9 0.8 fusion.87
  123.1 0.6 fusion.98
  123.7 0.5 slice_bitcast_fusion.13
  124.3 1.2 fusion.27
  125.8 0.4 fusion.172
  126.2 8.3 %collective-permute-start.4 = (f32[3,20,2,1024]{3,2,1,0:T(2,128)S(1)}, f32[3,20,2,1024]{3,2,1,0:T(2,128)S(1)}, u32[]{:S(2)}, u32[]{:S(2)}) collective-permute-start(f32[3,20,2,1024]{3,2,1,0:T(2,128)S(1)} %get-tuple-element.70), channel_id=1, source_target_pairs={{0,1},{1,2},{2,3},{4,5},{5,6},{6,7},{8,9},{9,10},{10,11},{12,13},{... | collective-permute-start | bytes 1474568 | tf_op jit(solution)/shard_map/ppermute | solution.py:24
  134.6 1.5 collective-permute-start.5
  136.1 2.2 %collective-permute-done.5 = f32[3,20,2,1024]{3,2,1,0:T(2,128)S(1)} collective-permute-done((f32[3,20,2,1024]{3,2,1,0:T(2,128)S(1)}, f32[3,20,2,1024]{3,2,1,0:T(2,128)S(1)}, u32[]{:S(2)}, u32[]{:S(2)}) %collective-permute-start.5) | collective-permute-done | bytes 491552 | tf_op jit(solution)/shard_map/ppermute | solution.py:26
  138.3 0.6 pad_maximum_fusion.2
  140.3 0.8 fusion.63
  141.5 0.6 fusion.74
  142.1 0.5 slice_bitcast_fusion.11
  143.6 0.9 pad_maximum_fusion.3
  144.6 1.3 fusion.2
  146.2 0.4 copy.49
  146.6 8.3 %collective-permute-start.6 = (f32[3,20,2,1024]{3,2,1,0:T(2,128)S(1)}, f32[3,20,2,1024]{3,2,1,0:T(2,128)S(1)}, u32[]{:S(2)}, u32[]{:S(2)}) collective-permute-start(f32[3,20,2,1024]{3,2,1,0:T(2,128)S(1)} %copy.49), channel_id=1, source_target_pairs={{0,1},{1,2},{2,3},{4,5},{5,6},{6,7},{8,9},{9,10},{10,11},{12,13},{... | collective-permute-start | bytes 1474568 | tf_op jit(solution)/shard_map/ppermute | solution.py:24
  154.9 0.4 copy.50
  155.3 1.6 collective-permute-start.7
  157.2 1.8 collective-permute-done.7
  159.4 2.1 %pad_maximum_fusion.12 = (f32[1,20,8,1024]{3,0,2,1:T(1,128)S(1)}, f32[1,20,8,1024]{3,0,2,1:T(1,128)S(1)}, f32[1,20,8,1024]{3,0,2,1:T(1,128)S(1)}) fusion(f32[3,20,2,1024]{3,0,2,1:T(4,128)S(1)} %copy.52, f32[3,20,4,1024]{3,0,2,1:T(4,128)S(1)} %fusion.2, f32[3,20,2,1024]{3,0,2,1:T(4,128)S(1)} %copy.51), kind=kLoop, calls=%fused_computation.74 | loop fusion | flops 983040 | bytes 3932160 | tf_op jit(solution)/shard_map/slice | solution.py:43
  163.0 0.8 fusion.39
  164.3 0.6 fusion.50
  165.1 1.0 fusion.138
  166.7 13.1 %psum.7 = f32[1]{0:T(128)} all-reduce(f32[1]{0:T(128)} %bitcast.38), channel_id=1, replica_groups=mesh['parts'=2,'member'=4,'tile'=4] {'tile'}, use_global_device_ids=true, to_apply=%region_2.3 | all-reduce | flops 1 | bytes 8 | tf_op jit(solution)/shard_map/psum | solution.py:112
  179.9 0.5 slice_bitcast_fusion.10
  180.4 1.2 maximum_bitcast_fusion
  (87 shorter events, 9.5 us)
Async XLA Ops:
  7.2 3.0 %copy-start.2 = (s32[4]{0:T(128)S(1)}, s32[4]{0:T(128)}, u32[]{:S(2)}) copy-start(s32[4]{0:T(128)} %param.15) | copy-start | bytes 52
  7.2 81.6 %all-gather.2.cloned.1.call-start = ((), (), s32[]{:S(2)}) async-start(), calls=%async_computation | async-start | bytes 4915200 | tf_op jit(solution)/shard_map/all_gather | solution.py:94
  11.4 81.0 %copy-start = (bf16[1,128,4096]{2,1,0:T(8,128)(2,1)S(1)}, bf16[1,128,4096]{2,1,0:T(8,128)(2,1)}, u32[]{:S(2)}) copy-start(bf16[1,128,4096]{2,1,0:T(8,128)(2,1)} %param.17) | copy-start | bytes 3145732
  11.5 81.0 %copy-start.1 = (f32[1,2,128]{2,1,0:T(2,128)S(1)}, f32[1,2,128]{2,1,0:T(2,128)}, u32[]{:S(2)}) copy-start(f32[1,2,128]{2,1,0:T(2,128)} %param.18) | copy-start | bytes 3076
  92.5 4.8 %copy-start.3 = (f32[20]{0:T(128)S(1)}, f32[20]{0:T(128)}, u32[]{:S(2)}) copy-start(f32[20]{0:T(128)} %param.16) | copy-start | bytes 244
  94.2 3.2 %collective-permute-start = (f32[3,20,2,1024]{3,2,1,0:T(2,128)S(1)}, f32[3,20,2,1024]{3,2,1,0:T(2,128)S(1)}, u32[]{:S(2)}, u32[]{:S(2)}) collective-permute-start(f32[3,20,2,1024]{3,2,1,0:T(2,128)S(1)} %get-tuple-element.74), channel_id=1, source_target_pairs={{0,1},{1,2},{2,3},{4,5},{5,6},{6,7},{8,9},{9,10},{10,11},{12,13},{... | collective-permute-start | bytes 1474568 | tf_op jit(solution)/shard_map/ppermute | solution.py:24
  96.0 5.0 %collective-permute-start.1 = (f32[3,20,2,1024]{3,2,1,0:T(2,128)S(1)}, f32[3,20,2,1024]{3,2,1,0:T(2,128)S(1)}, u32[]{:S(2)}, u32[]{:S(2)}) collective-permute-start(f32[3,20,2,1024]{3,2,1,0:T(2,128)S(1)} %get-tuple-element.75), channel_id=1, source_target_pairs={{1,0},{2,1},{3,2},{5,4},{6,5},{7,6},{9,8},{10,9},{11,10},{13,12},{... | collective-permute-start | bytes 1474568 | tf_op jit(solution)/shard_map/ppermute | solution.py:26
  107.3 10.3 %collective-permute-start.2 = (f32[3,20,2,1024]{3,2,1,0:T(2,128)S(1)}, f32[3,20,2,1024]{3,2,1,0:T(2,128)S(1)}, u32[]{:S(2)}, u32[]{:S(2)}) collective-permute-start(f32[3,20,2,1024]{3,2,1,0:T(2,128)S(1)} %get-tuple-element.72), channel_id=1, source_target_pairs={{0,1},{1,2},{2,3},{4,5},{5,6},{6,7},{8,9},{9,10},{10,11},{12,13},{... | collective-permute-start | bytes 1474568 | tf_op jit(solution)/shard_map/ppermute | solution.py:24
  116.1 3.8 %collective-permute-start.3 = (f32[3,20,2,1024]{3,2,1,0:T(2,128)S(1)}, f32[3,20,2,1024]{3,2,1,0:T(2,128)S(1)}, u32[]{:S(2)}, u32[]{:S(2)}) collective-permute-start(f32[3,20,2,1024]{3,2,1,0:T(2,128)S(1)} %get-tuple-element.73), channel_id=1, source_target_pairs={{1,0},{2,1},{3,2},{5,4},{6,5},{7,6},{9,8},{10,9},{11,10},{13,12},{... | collective-permute-start | bytes 1474568 | tf_op jit(solution)/shard_map/ppermute | solution.py:26
  126.2 9.8 %collective-permute-start.4 = (f32[3,20,2,1024]{3,2,1,0:T(2,128)S(1)}, f32[3,20,2,1024]{3,2,1,0:T(2,128)S(1)}, u32[]{:S(2)}, u32[]{:S(2)}) collective-permute-start(f32[3,20,2,1024]{3,2,1,0:T(2,128)S(1)} %get-tuple-element.70), channel_id=1, source_target_pairs={{0,1},{1,2},{2,3},{4,5},{5,6},{6,7},{8,9},{9,10},{10,11},{12,13},{... | collective-permute-start | bytes 1474568 | tf_op jit(solution)/shard_map/ppermute | solution.py:24
  134.6 3.8 %collective-permute-start.5 = (f32[3,20,2,1024]{3,2,1,0:T(2,128)S(1)}, f32[3,20,2,1024]{3,2,1,0:T(2,128)S(1)}, u32[]{:S(2)}, u32[]{:S(2)}) collective-permute-start(f32[3,20,2,1024]{3,2,1,0:T(2,128)S(1)} %get-tuple-element.71), channel_id=1, source_target_pairs={{1,0},{2,1},{3,2},{5,4},{6,5},{7,6},{9,8},{10,9},{11,10},{13,12},{... | collective-permute-start | bytes 1474568 | tf_op jit(solution)/shard_map/ppermute | solution.py:26
  146.6 10.3 %collective-permute-start.6 = (f32[3,20,2,1024]{3,2,1,0:T(2,128)S(1)}, f32[3,20,2,1024]{3,2,1,0:T(2,128)S(1)}, u32[]{:S(2)}, u32[]{:S(2)}) collective-permute-start(f32[3,20,2,1024]{3,2,1,0:T(2,128)S(1)} %copy.49), channel_id=1, source_target_pairs={{0,1},{1,2},{2,3},{4,5},{5,6},{6,7},{8,9},{9,10},{10,11},{12,13},{... | collective-permute-start | bytes 1474568 | tf_op jit(solution)/shard_map/ppermute | solution.py:24
  155.3 3.8 %collective-permute-start.7 = (f32[3,20,2,1024]{3,2,1,0:T(2,128)S(1)}, f32[3,20,2,1024]{3,2,1,0:T(2,128)S(1)}, u32[]{:S(2)}, u32[]{:S(2)}) collective-permute-start(f32[3,20,2,1024]{3,2,1,0:T(2,128)S(1)} %copy.50), channel_id=1, source_target_pairs={{1,0},{2,1},{3,2},{5,4},{6,5},{7,6},{9,8},{10,9},{11,10},{13,12},{... | collective-permute-start | bytes 1474568 | tf_op jit(solution)/shard_map/ppermute | solution.py:26
Sparse Core Ops, SparseCore 0:
  9.6 79.1 all-gather.1
where the time goes:
time: 189 us; the launch traced here: 188 us
  waiting for transfers between devices  88 us (47%)
  starting transfers between devices  33.1 us (18%)
  other arithmetic  18.8 us (10%)
  between operations  16.1 us (9%)
  local copies, waits for them, and re-layouts  13.3 us (7%)
  blocking collectives  13.1 us (7%)
  matrix products  6.03 us (3%)
    all_gather x1, waiting for transfers between devices, per_device(): piece = lax.all_gather(state, 'member', axis=0, tiled=True)  77.3 us
    ppermute x4, starting transfers between devices, with_halo(): lax.ppermute(tail, axis, [(i, (i + 1) % count) for i in range(ends)])  27.2 us
    psum x1, blocking collectives, per_device(): total = lax.psum(0.5 * jnp.sum(innov * innov), 'tile')  13.1 us
    ppermute x4, waiting for transfers between devices, with_halo(): lax.ppermute(head, axis, [((i + 1) % count, i) for i in range(ends)])  9.9 us
    ppermute x4, starting transfers between devices, with_halo(): lax.ppermute(head, axis, [((i + 1) % count, i) for i in range(ends)])  5.83 us
    slice x30, local copies, waits for them, and re-layouts, shift_cols(): return jnp.roll(field, nudge_quantity, axis=2)  5.53 us
    dot_general x4, matrix products, per_device(): jnp.dot(innov.astype(jnp.bfloat16), coefficient_array, preferred_element_...  5.04 us
  transfers between devices with their start and end apart: 9, of which 6 were waited for; matrix products, arithmetic and copies ran while one was open for 2% of the time, Pallas kernels for 0%

commit v1 on v0

v1 whole, which is shorter than its diff:
```python
import functools

import jax
import jax.numpy as jnp
from jax import lax
from jax.experimental import pallas as pl
from jax.experimental.pallas import tpu as pltpu
from jax.sharding import PartitionSpec as P

STEPS = 4
U, H, V = 0, 1, 2
SOURCE = {U: 0, V: 1, H: 2}
MESH = pl.DeviceIdType.MESH

time_step = 0.3
nudge_gain = 2.0
coriolis = 0.5
viscosity = 0.05
mixing = 0.1


def west(field):
    turned = pltpu.roll(field, 1, 2)
    wrapped = pltpu.roll(turned, 1, 1)
    lane = lax.broadcasted_iota(jnp.int32, field.shape, 2)
    return jnp.where(lane == 0, wrapped, turned)


def east(field):
    turned = pltpu.roll(field, 127, 2)
    wrapped = pltpu.roll(turned, 7, 1)
    lane = lax.broadcasted_iota(jnp.int32, field.shape, 2)
    return jnp.where(lane == 127, wrapped, turned)


def forecast_kernel(
    levels, tiles,
    state, depth, interp, obs, counts,
    out, misfit,
    x, terms, send_sem, recv_sem, term_send, term_recv,
):
    tile = lax.axis_index("tile")
    right, left = lax.rem(tile + 1, tiles), lax.rem(tile + tiles - 1, tiles)
    barrier = pltpu.get_barrier_semaphore()
    for hop in range(1, tiles):
        pl.semaphore_signal(
            barrier, inc=1, device_id={"tile": lax.rem(tile + hop, tiles)}, device_id_type=MESH
        )

    split = [levels // 2 - 1 + t for t in range(STEPS + 1)]

    def span(group, t):
        return (split[t], levels) if group == 0 else (0, split[t])

    def raw(f, l, r):
        return pl.ds((SOURCE[f] * levels + l) * 32 + r, 8, stride=4)

    def load(group):
        low, high = span(group, 0)

        @pl.loop(low, high)
        def _(l):
            for f in (U, H, V):
                for r in range(4):
                    x[0, f, l, 2 + r] = state[raw(f, l, r), :]

    def halo(group, t, side):
        low, high = span(group, t)
        lv = pl.ds(low, high - low)
        if side == 0:
            pieces = ((x.at[t, pl.ds(0, 2), lv, pl.ds(4, 2)], x.at[t, pl.ds(0, 2), lv, pl.ds(0, 2)]),
                      (x.at[t, V, lv, pl.ds(5, 1)], x.at[t, V, lv, pl.ds(1, 1)]))
            to = right
        else:
            pieces = ((x.at[t, pl.ds(0, 2), lv, pl.ds(2, 2)], x.at[t, pl.ds(0, 2), lv, pl.ds(6, 2)]),
                      (x.at[t, V, lv, pl.ds(2, 1)], x.at[t, V, lv, pl.ds(6, 1)]))
            to = left
        return [
            pltpu.make_async_remote_copy(
                src_ref=src, dst_ref=dst,
                send_sem=send_sem.at[t, group, side, i], recv_sem=recv_sem.at[t, group, side, i],
                device_id={"tile": to}, device_id_type=MESH,
            )
            for i, (src, dst) in enumerate(pieces)
        ]

    sends = (tile < tiles - 1, tile > 0)
    receives = (tile > 0, tile < tiles - 1)

    def send(group, t):
        for side in (0, 1):
            @pl.when(sends[side])
            def _():
                for copy in halo(group, t, side):
                    copy.start()

    def arrived(group, t):
        for side in (0, 1):
            @pl.when(receives[side])
            def _():
                for copy in halo(group, t, side):
                    copy.wait_recv()

    def cell(t, l, below, above):
        u, h = x[t, U, l], x[t, H, l]
        v = x[t, V, l, 1:7]
        core = u[1:7]
        u1 = (
            (1.0 - time_step * (4.0 * viscosity + 2.0 * mixing)) * core
            + (time_step * coriolis) * v
            - (time_step * 0.5) * (h[2:8] - h[0:6])
            + (time_step * viscosity) * ((u[2:8] + u[0:6]) + (west(core) + east(core)))
            + (time_step * mixing) * (x[t, U, below, 1:7] + x[t, U, above, 1:7])
        )
        mid = v[1:5]
        diffuse = (time_step * viscosity) * mid
        slope = (time_step * 0.5) * h[2:6]
        v1 = (
            (1.0 - time_step * (4.0 * viscosity + 2.0 * mixing)) * mid
            - (time_step * coriolis) * u[2:6]
            + (time_step * viscosity) * (v[2:6] + v[0:4])
            + (east(diffuse - slope) + west(diffuse + slope))
            + (time_step * mixing) * (x[t, V, below, 2:6] + x[t, V, above, 2:6])
        )
        h1 = h[2:6] - (time_step * 0.5 * depth[l]) * (
            (u1[2:6] - u1[0:4]) + (east(v1) - west(v1))
        )
        x[t + 1, U, l, 2:6] = u1[1:5]
        x[t + 1, V, l, 2:6] = v1
        x[t + 1, H, l, 2:6] = h1

    def advance(group, t):
        low, high = span(group, t + 1)
        if low == 0:
            cell(t, 0, 0, 1)
            low = 1
        last = high == levels
        if last:
            high = levels - 1

        @pl.loop(low, high)
        def _(l):
            cell(t, l, l - 1, l + 1)

        if last:
            cell(t, levels - 1, levels - 2, levels - 1)

    row = lax.broadcasted_iota(jnp.int32, (8, 128), 0)
    live = lax.broadcasted_iota(jnp.int32, (1, 128), 1) < counts[0]

    def residual(t):
        pieces = []
        for r in range(4):
            u, v = x[t, U, 0, 2 + r], x[t, V, 0, 2 + r]
            for block in range(8):
                here = row == block
                pieces.append(
                    jnp.concatenate([jnp.where(here, u, 0.0), jnp.where(here, v, 0.0)], axis=0)
                    .astype(jnp.bfloat16)
                )
        surf = jnp.concatenate(pieces, axis=1)
        pred = lax.dot_general(
            surf, interp[...], (((1,), (1,)), ((), ())), preferred_element_type=jnp.float32
        )
        result = []
        for k in (0, 1):
            whole = jnp.sum(pred[8 * k:8 * k + 8], axis=0, keepdims=True)
            result.append(jnp.where(live, obs[k:k + 1, :] - whole, 0.0))
        return result

    def nudge(t):
        innov = jnp.concatenate(
            [jnp.broadcast_to(part, (8, 128)) for part in residual(t)], axis=0
        ).astype(jnp.bfloat16)
        back = jnp.dot(innov, interp[...], preferred_element_type=jnp.float32)
        for k, f in ((0, U), (1, V)):
            for r in range(4):
                total = jnp.zeros((8, 128), jnp.float32)
                for block in range(8):
                    at = (r * 8 + block) * 128
                    total = jnp.where(row == block, back[8 * k:8 * k + 8, at:at + 128], total)
                x[t, f, 0, 2 + r] += (time_step * nudge_gain) * total

    def store(group):
        low, high = span(group, STEPS)

        @pl.loop(low, high)
        def _(l):
            for f in (U, H, V):
                for r in range(4):
                    out[raw(f, l, r), :] = x[STEPS, f, l, 2 + r]

    for side, rows in ((0, 0), (1, 6)):
        @pl.when(jnp.logical_not(receives[side]))
        def _():
            @pl.loop(0, levels)
            def _(l):
                for t in range(STEPS):
                    for f in (U, H, V):
                        x[t, f, l, rows:rows + 2] = jnp.zeros((2, 8, 128), jnp.float32)

    load(0)
    pl.semaphore_wait(barrier, tiles - 1)
    send(0, 0)
    load(1)
    nudge(0)
    send(1, 0)
    for t in range(STEPS):
        for group in (0, 1):
            arrived(group, t)
            advance(group, t)
            if t + 1 < STEPS:
                if group == 1:
                    nudge(t + 1)
                send(group, t + 1)
            else:
                store(group)

    part_u, part_v = residual(STEPS)
    terms[pl.ds(tile, 1)] = jnp.broadcast_to(
        0.5 * (part_u * part_u + part_v * part_v), (1, 8, 128)
    )
    copies = []
    for hop in range(1, tiles):
        copies.append((
            pltpu.make_async_remote_copy(
                src_ref=terms.at[tile], dst_ref=terms.at[tile],
                send_sem=term_send.at[hop], recv_sem=term_recv.at[hop],
                device_id={"tile": lax.rem(tile + hop, tiles)}, device_id_type=MESH,
            ),
            pltpu.make_async_remote_copy(
                src_ref=terms.at[tile], dst_ref=terms.at[lax.rem(tile + tiles - hop, tiles)],
                send_sem=term_send.at[hop], recv_sem=term_recv.at[hop],
                device_id={"tile": lax.rem(tile + hop, tiles)}, device_id_type=MESH,
            ),
        ))
    for copy, _ in copies:
        copy.start()
    for t in range(STEPS):
        for group in (0, 1):
            for side in (0, 1):
                @pl.when(sends[side])
                def _():
                    for copy in halo(group, t, side):
                        copy.wait_send()
    for copy, arrival in copies:
        copy.wait_send()
        arrival.wait_recv()
    total = terms[0, 0:1]
    for other in range(1, tiles):
        total = total + terms[other, 0:1]
    misfit[0] = jnp.sum(total)


def per_device(tiles, state, parent, depth, interp, obs, counts):
    _, fields, levels, rows, cols = state.shape
    blocks = cols // 128
    tall = fields * levels * rows * blocks
    raw = state.reshape(fields * levels, rows, blocks, 128).transpose(0, 2, 1, 3).reshape(tall, 128)
    vmem, smem = pl.BlockSpec(memory_space=pltpu.VMEM), pl.BlockSpec(memory_space=pltpu.SMEM)
    forecast, misfit = pl.pallas_call(
        functools.partial(forecast_kernel, levels, tiles),
        out_shape=(
            jax.ShapeDtypeStruct((tall, 128), jnp.float32),
            jax.ShapeDtypeStruct((1,), jnp.float32),
        ),
        in_specs=[vmem, smem, vmem, vmem, smem],
        out_specs=(vmem, smem),
        scratch_shapes=[
            pltpu.VMEM((STEPS + 1, fields, levels, rows + 4, blocks, 128), jnp.float32),
            pltpu.VMEM((tiles, 8, 128), jnp.float32),
            pltpu.SemaphoreType.DMA((STEPS, 2, 2, 2)),
            pltpu.SemaphoreType.DMA((STEPS, 2, 2, 2)),
            pltpu.SemaphoreType.DMA((tiles,)),
            pltpu.SemaphoreType.DMA((tiles,)),
        ],
        compiler_params=pltpu.CompilerParams(
            collective_id=0, has_side_effects=True, vmem_limit_bytes=40 << 20
        ),
    )(raw, depth, interp[0], obs[0], counts)

    mine = parent[lax.axis_index("member")]
    everyone = lax.all_gather(forecast, "member", axis=0)
    selected = jnp.arange(everyone.shape[0], dtype=jnp.int32) == mine
    chosen = jnp.sum(jnp.where(selected[:, None, None], everyone, 0.0), axis=0)
    misfits = lax.all_gather(misfit, "member", axis=0, tiled=True)
    chosen_misfit = jnp.sum(jnp.where(selected, misfits, 0.0))
    result = chosen.reshape(fields * levels, blocks, rows, 128).transpose(0, 2, 1, 3)
    return result.reshape(state.shape), chosen_misfit.reshape(1)


def solution(mesh):
    return jax.shard_map(
        functools.partial(per_device, mesh.shape["tile"]),
        mesh=mesh,
        in_specs=(
            P(("parts", "member"), None, None, "tile", None),
            P("parts"),
            P(),
            P(("parts", "tile"), None, None),
            P(("parts", "tile"), None, None),
            P(("parts", "tile")),
        ),
        out_specs=(P(("parts", "member"), None, None, "tile", None), P(("parts", "member"))),
        check_vma=False,
    )
```

time: 189 us -> 138 us (0.73)
  Pallas kernels: 0 us -> 38.1 us
  starting transfers between devices: 33.1 us -> 0.04 us
  waiting for transfers between devices: 88 us -> 59.5 us
  other arithmetic: 18.8 us -> 5.39 us
  matrix products: 6.03 us -> 0 us
  local copies, waits for them, and re-layouts: 13.3 us -> 7.53 us
    pallas_call x0 -> x1, Pallas kernels: none -> 38.1 us  [per_device(): pl.pallas_call(functools.partial(forecast_kernel, levels, tiles), out_sha...]
    ppermute x8 -> x0, starting transfers between devices: 33.1 us -> none  [the longest x4 27.2 us: with_halo(): lax.ppermute(tail, axis, [(i, (i + 1) % count) for i in range(ends)])]
    all_gather x1, waiting for transfers between devices: 77.3 us -> 59.5 us  [per_device(): everyone = lax.all_gather(forecast, 'member', axis=0)]
    psum x1 -> x0, blocking collectives: 13.1 us -> none  [per_device(): total = lax.psum(0.5 * jnp.sum(innov * innov), 'tile')]
    unnamed x0 -> x1, blocking collectives: none -> 12.5 us
    ppermute x8 -> x0, waiting for transfers between devices: 10 us -> none  [the longest x4 9.9 us: with_halo(): lax.ppermute(head, axis, [((i + 1) % count, i) for i in range(ends)])]
    slice x48 -> x0, local copies, waits for them, and re-layouts: 8.18 us -> none  [the longest x30 5.53 us: shift_cols(): return jnp.roll(field, nudge_quantity, axis=2)]
    dot_general x5 -> x0, matrix products: 6.03 us -> none  [the longest x4 5.04 us: per_device(): jnp.dot(innov.astype(jnp.bfloat16), coefficient_array, preferred_element_...]
  transfers between devices with their start and end apart: 9 -> 1, of which waited for: 6 -> 1; matrix products, arithmetic and copies ran while one was open for 2% -> 4% of each run, Pallas kernels for 0% -> 0%
where the time goes in v1:
time: 138 us
  waiting for transfers between devices  59.5 us (43%)
  Pallas kernels  38.1 us (28%)
  between operations  14.7 us (11%)
  blocking collectives  12.5 us (9%)
  local copies, waits for them, and re-layouts  7.53 us (5%)
  other arithmetic  5.39 us (4%)
    all_gather x1, waiting for transfers between devices, per_device(): everyone = lax.all_gather(forecast, 'member', axis=0)  59.5 us
    pallas_call x1, Pallas kernels, per_device(): pl.pallas_call(functools.partial(forecast_kernel, levels, tiles), out_sha...  38.1 us
    unnamed x1, blocking collectives  12.5 us
    unnamed x11, local copies, waits for them, and re-layouts  6.3 us
    reduce_sum x1, other arithmetic, per_device(): chosen = jnp.sum(jnp.where(selected[:, None, None], everyone, 0.0), axis=0)  3.5 us
  transfers between devices with their start and end apart: 1, of which 1 were waited for; matrix products, arithmetic and copies ran while one was open for 4% of the time, Pallas kernels for 0%

profile of v1, /device:TPU:0, one launch (start us, length us, event | category | flops | bytes accessed | tf_op | source)
XLA Modules:
  0.0 137.9 jit_solution(16207571325969269771)
XLA Ops:
  7.2 0.0 all-gather.3.cloned.1.call-start
  7.9 0.0 copy-start
  7.9 1.2 copy-done
  9.1 0.0 copy-start.1
  9.1 1.2 copy-done.1
  10.3 0.0 copy-start.2
  10.3 0.7 copy-done.2
  11.0 0.0 copy-start.3
  11.0 0.7 copy-done.3
  11.6 38.1 %shard_map.77 = (f32[1920,128]{1,0:T(8,128)}, f32[1]{0:T(128)}) custom-call(f32[1920,128]{1,0:T(8,128)S(1)} %bitcast.17, f32[20]{0:T(128)S(1)} %copy-done.3, bf16[128,4096]{1,0:T(8,128)(2,1)S(1)} %bitcast.16, f32[2,128]{1,0:T(2,128)S(1)} %bitcast.18, s32[1]{0:T(128)S(6)} %copy.11.counts), custom_call_target="tpu_custom_call" | custom-call | tf_op jit(solution)/shard_map/pallas_call | solution.py:261
  49.8 0.0 all-gather.3.cloned.1.call-update
  49.8 1.2 dynamic-slice
  51.0 1.3 dynamic-update-slice
  52.3 12.5 %all-reduce = f32[4]{0:T(128)S(1)} all-reduce(f32[4]{0:T(128)S(1)} %dynamic-update-slice), channel_id=1, replica_groups=mesh['parts'=2,'member'=4,'tile'=4] {'member'}, use_global_device_ids=true, to_apply=%add | all-reduce | flops 4 | bytes 32
  64.9 1.2 dynamic_slice.3
  66.1 0.6 iota_compare_fusion
  66.8 1.2 select_reduce_fusion.1
  68.0 59.5 %all-gather.3.cloned.1.call-done = f32[7680,128]{1,0:T(8,128)} async-done(((f32[1920,128]{1,0:T(8,128)}), f32[7680,128]{1,0:T(8,128)}) %all-gather.3.cloned.1.call-update) | async-done | bytes 3932176 | tf_op jit(solution)/shard_map/all_gather | solution.py:283
  127.5 3.5 %select_reduce_fusion = f32[1920,128]{1,0:T(8,128)} fusion(f32[4,1920,128]{2,1,0:T(8,128)} %bitcast.19, pred[4]{0:T(512)(128)(4,1)S(1)} %iota_compare_fusion), kind=kLoop, calls=%fused_computation | loop fusion | flops 1720320 | bytes 4915204 | tf_op jit(solution)/shard_map/reduce_sum | solution.py:285
  (1 shorter events, 0.0 us)
Async XLA Ops:
  7.2 120.4 %all-gather.3.cloned.1.call-start = ((), (), s32[]{:S(2)}) async-start(), calls=%async_computation | async-start | bytes 4915200 | tf_op jit(solution)/shard_map/all_gather | solution.py:283
  7.9 1.2 copy-start
  9.1 1.2 copy-start.1
  10.3 0.7 copy-start.2
  11.0 0.7 copy-start.3
Sparse Core Ops, SparseCore 0:
  49.9 77.5 all-gather.2

commit v2 on v1

--- a/solution.py
+++ b/solution.py
@@ -8,6 +8,7 @@
 from jax.sharding import PartitionSpec as P
 
 STEPS = 4
+GROUPS = 4
 U, H, V = 0, 1, 2
 SOURCE = {U: 0, V: 1, H: 2}
 MESH = pl.DeviceIdType.MESH
@@ -34,10 +35,12 @@
 
 
 def forecast_kernel(
-    levels, tiles,
-    state, depth, interp, obs, counts,
+    levels, tiles, members,
+    state, parent, depth, interp, obs, counts,
     out, misfit,
-    x, terms, send_sem, recv_sem, term_send, term_recv,
+    x, done, inbox, outbox, terms, member_terms,
+    send_sem, recv_sem, ship_send, ship_recv,
+    term_send, term_recv, member_send, member_recv,
 ):
     tile = lax.axis_index("tile")
     right, left = lax.rem(tile + 1, tiles), lax.rem(tile + tiles - 1, tiles)
@@ -47,10 +50,18 @@
             barrier, inc=1, device_id={"tile": lax.rem(tile + hop, tiles)}, device_id_type=MESH
         )
 
-    split = [levels // 2 - 1 + t for t in range(STEPS + 1)]
+    me = lax.axis_index("member")
+    for hop in range(1, members):
+        pl.semaphore_signal(
+            barrier, inc=1, device_id={"member": lax.rem(me + hop, members)}, device_id_type=MESH
+        )
+
+    ends = [levels * (GROUPS - g) // GROUPS for g in range(GROUPS + 1)]
 
     def span(group, t):
-        return (split[t], levels) if group == 0 else (0, split[t])
+        low = 0 if group == GROUPS - 1 else ends[group + 1] - STEPS + t
+        high = levels if group == 0 else ends[group] - STEPS + t
+        return low, high
 
     def raw(f, l, r):
         return pl.ds((SOURCE[f] * levels + l) * 32 + r, 8, stride=4)
@@ -125,9 +136,14 @@
         h1 = h[2:6] - (time_step * 0.5 * depth[l]) * (
             (u1[2:6] - u1[0:4]) + (east(v1) - west(v1))
         )
-        x[t + 1, U, l, 2:6] = u1[1:5]
-        x[t + 1, V, l, 2:6] = v1
-        x[t + 1, H, l, 2:6] = h1
+        if t + 1 < STEPS:
+            x[t + 1, U, l, 2:6] = u1[1:5]
+            x[t + 1, V, l, 2:6] = v1
+            x[t + 1, H, l, 2:6] = h1
+        else:
+            done[U, l] = u1[1:5]
+            done[V, l] = v1
+            done[H, l] = h1
 
     def advance(group, t):
         low, high = span(group, t + 1)
@@ -151,7 +167,10 @@
     def residual(t):
         pieces = []
         for r in range(4):
-            u, v = x[t, U, 0, 2 + r], x[t, V, 0, 2 + r]
+            if t < STEPS:
+                u, v = x[t, U, 0, 2 + r], x[t, V, 0, 2 + r]
+            else:
+                u, v = done[U, 0, r], done[V, 0, r]
             for block in range(8):
                 here = row == block
                 pieces.append(
@@ -181,14 +200,119 @@
                     total = jnp.where(row == block, back[8 * k:8 * k + 8, at:at + 128], total)
                 x[t, f, 0, 2 + r] += (time_step * nudge_gain) * total
 
-    def store(group):
+    half = members // 2
+    place = (me, members - 1 - me)
+    following = (lax.rem(me + 1, members), lax.rem(me + members - 1, members))
+
+    def parent_place(way, place_of):
+        return parent[place_of] if way == 0 else members - 1 - parent[members - 1 - place_of]
+
+    def is_value(value, number):
+        return jnp.broadcast_to((jnp.full((8, 128), value, jnp.int32) == number)[None], (4, 8, 128))
+
+    def ship(way, source, slot, group):
         low, high = span(group, STEPS)
+        lv = pl.ds(low, high - low)
+        return pltpu.make_async_remote_copy(
+            src_ref=source.at[:, lv], dst_ref=inbox.at[way, slot, :, lv],
+            send_sem=ship_send.at[way, slot, group], recv_sem=ship_recv.at[way, slot, group],
+            device_id={"member": following[way]}, device_id_type=MESH,
+        )
+
+    def ship_own(group):
+        for way in (0, 1):
+            @pl.when(place[way] < half)
+            def _():
+                ship(way, done, place[way], group).start()
+
+    def relay(group):
+        for way in (0, 1):
+            @pl.when(place[way] < half)
+            def _():
+                @pl.loop(0, place[way])
+                def _(slot):
+                    ship(way, done, slot, group).wait_recv()
+                    ship(way, inbox.at[way, slot], slot, group).start()
+
+    def take(group):
+        low, high = span(group, STEPS)
+        for way in (0, 1):
+            @pl.when(place[way] == half)
+            def _():
+                @pl.loop(0, half)
+                def _(slot):
+                    ship(way, done, slot, group).wait_recv()
+
+                @pl.loop(half + 1, members)
+                def _(receiver):
+                    wanted = parent_place(way, receiver)
+                    slot = receiver - half - 1
+                    masks = [is_value(wanted, other) for other in range(half)]
+
+                    @pl.loop(low, high)
+                    def _(l):
+                        for f in (U, H, V):
+                            value = done[f, l]
+                            for other in range(half):
+                                value = jnp.where(masks[other], inbox[way, other, f, l], value)
+                            outbox[way, slot, f, l] = value
+
+                    ship(way, outbox.at[way, slot], slot, group).start()
+
+            @pl.when(place[way] > half)
+            def _():
+                @pl.loop(place[way], members)
+                def _(receiver):
+                    ship(way, done, receiver - half - 1, group).wait_recv()
+
+                @pl.loop(place[way] + 1, members)
+                def _(receiver):
+                    slot = receiver - half - 1
+                    own = is_value(parent_place(way, receiver), place[way])
+
+                    @pl.loop(low, high)
+                    def _(l):
+                        for f in (U, H, V):
+                            outbox[way, slot, f, l] = jnp.where(
+                                own, done[f, l], inbox[way, slot, f, l]
+                            )
+
+                    ship(way, outbox.at[way, slot], slot, group).start()
+
+    def finish(group):
+        low, high = span(group, STEPS)
+        masks = []
+        for way in (0, 1):
+            wanted = parent_place(way, place[way])
+            slot = jnp.where(
+                wanted < place[way],
+                jnp.where(place[way] <= half, wanted, place[way] - half - 1),
+                -1,
+            )
+            masks += [(way, other, is_value(slot, other)) for other in range(half)]
 
         @pl.loop(low, high)
         def _(l):
             for f in (U, H, V):
+                value = done[f, l]
+                for way, other, mask in masks:
+                    value = jnp.where(mask, inbox[way, other, f, l], value)
                 for r in range(4):
-                    out[raw(f, l, r), :] = x[STEPS, f, l, 2 + r]
+                    out[raw(f, l, r), :] = value[r]
+
+    def shipped(group):
+        for way in (0, 1):
+            @pl.when(place[way] < half)
+            def _():
+                @pl.loop(0, place[way] + 1)
+                def _(slot):
+                    ship(way, done, slot, group).wait_send()
+
+            @pl.when(place[way] >= half)
+            def _():
+                @pl.loop(place[way] + 1, members)
+                def _(receiver):
+                    ship(way, done, receiver - half - 1, group).wait_send()
 
     for side, rows in ((0, 0), (1, 6)):
         @pl.when(jnp.logical_not(receives[side]))
@@ -200,21 +324,29 @@
                         x[t, f, l, rows:rows + 2] = jnp.zeros((2, 8, 128), jnp.float32)
 
     load(0)
-    pl.semaphore_wait(barrier, tiles - 1)
+    pl.semaphore_wait(barrier, tiles + members - 2)
     send(0, 0)
-    load(1)
-    nudge(0)
-    send(1, 0)
-    for t in range(STEPS):
-        for group in (0, 1):
-            arrived(group, t)
-            advance(group, t)
-            if t + 1 < STEPS:
-                if group == 1:
-                    nudge(t + 1)
-                send(group, t + 1)
-            else:
-                store(group)
+    for group in range(1, GROUPS):
+        load(group)
+        if group == GROUPS - 1:
+            nudge(0)
+        send(group, 0)
+    last = GROUPS + STEPS - 1
+    for stage in range(last):
+        for group in range(GROUPS):
+            t = stage - group
+            if 0 <= t < STEPS:
+                arrived(group, t)
+                advance(group, t)
+                if t + 1 < STEPS:
+                    if group == GROUPS - 1:
+                        nudge(t + 1)
+                    send(group, t + 1)
+                else:
+                    ship_own(group)
+        ready = stage - STEPS - 1
+        if ready >= 0:
+            relay(ready)
 
     part_u, part_v = residual(STEPS)
     terms[pl.ds(tile, 1)] = jnp.broadcast_to(
@@ -236,62 +368,87 @@
         ))
     for copy, _ in copies:
         copy.start()
-    for t in range(STEPS):
-        for group in (0, 1):
-            for side in (0, 1):
-                @pl.when(sends[side])
-                def _():
-                    for copy in halo(group, t, side):
-                        copy.wait_send()
+    for group in range(last - STEPS - 1, GROUPS):
+        relay(group)
     for copy, arrival in copies:
         copy.wait_send()
         arrival.wait_recv()
     total = terms[0, 0:1]
     for other in range(1, tiles):
         total = total + terms[other, 0:1]
-    misfit[0] = jnp.sum(total)
-
-
-def per_device(tiles, state, parent, depth, interp, obs, counts):
+    member_terms[pl.ds(me, 1)] = jnp.broadcast_to(total, (1, 8, 128))
+    copies = []
+    for hop in range(1, members):
+        for origin in (me, lax.rem(me + members - hop, members)):
+            copies.append(pltpu.make_async_remote_copy(
+                src_ref=member_terms.at[me], dst_ref=member_terms.at[origin],
+                send_sem=member_send.at[hop], recv_sem=member_recv.at[hop],
+                device_id={"member": lax.rem(me + hop, members)}, device_id_type=MESH,
+            ))
+    for copy in copies[::2]:
+        copy.start()
+    for group in range(GROUPS):
+        take(group)
+        finish(group)
+    for copy, arrival in zip(copies[::2], copies[1::2]):
+        copy.wait_send()
+        arrival.wait_recv()
+    chosen = jnp.zeros((8, 128), jnp.float32)
+    for other in range(members):
+        mask = jnp.full((8, 128), parent[me], jnp.int32) == other
+        chosen = jnp.where(mask, member_terms[other], chosen)
+    misfit[0] = jnp.sum(chosen[0:1])
+    for t in range(STEPS):
+        for group in range(GROUPS):
+            for side in (0, 1):
+                @pl.when(sends[side])
+                def _():
+                    for copy in halo(group, t, side):
+                        copy.wait_send()
+    for group in range(GROUPS):
+        shipped(group)
+
+
+def per_device(tiles, members, state, parent, depth, interp, obs, counts):
     _, fields, levels, rows, cols = state.shape
     blocks = cols // 128
     tall = fields * levels * rows * blocks
+    half = members // 2
     raw = state.reshape(fields * levels, rows, blocks, 128).transpose(0, 2, 1, 3).reshape(tall, 128)
     vmem, smem = pl.BlockSpec(memory_space=pltpu.VMEM), pl.BlockSpec(memory_space=pltpu.SMEM)
-    forecast, misfit = pl.pallas_call(
-        functools.partial(forecast_kernel, levels, tiles),
+    whole = (fields, levels, rows, blocks, 128)
+    dma = pltpu.SemaphoreType.DMA
+    result, misfit = pl.pallas_call(
+        functools.partial(forecast_kernel, levels, tiles, members),
         out_shape=(
             jax.ShapeDtypeStruct((tall, 128), jnp.float32),
             jax.ShapeDtypeStruct((1,), jnp.float32),
         ),
-        in_specs=[vmem, smem, vmem, vmem, smem],
+        in_specs=[vmem, smem, smem, vmem, vmem, smem],
         out_specs=(vmem, smem),
         scratch_shapes=[
-            pltpu.VMEM((STEPS + 1, fields, levels, rows + 4, blocks, 128), jnp.float32),
+            pltpu.VMEM((STEPS, fields, levels, rows + 4, blocks, 128), jnp.float32),
+            pltpu.VMEM(whole, jnp.float32),
+            pltpu.VMEM((2, half) + whole, jnp.float32),
+            pltpu.VMEM((2, max(half - 1, 1)) + whole, jnp.float32),
             pltpu.VMEM((tiles, 8, 128), jnp.float32),
-            pltpu.SemaphoreType.DMA((STEPS, 2, 2, 2)),
-            pltpu.SemaphoreType.DMA((STEPS, 2, 2, 2)),
-            pltpu.SemaphoreType.DMA((tiles,)),
-            pltpu.SemaphoreType.DMA((tiles,)),
+            pltpu.VMEM((members, 8, 128), jnp.float32),
+            dma((STEPS, GROUPS, 2, 2)), dma((STEPS, GROUPS, 2, 2)),
+            dma((2, half, GROUPS)), dma((2, half, GROUPS)),
+            dma((tiles,)), dma((tiles,)),
+            dma((members,)), dma((members,)),
         ],
         compiler_params=pltpu.CompilerParams(
-            collective_id=0, has_side_effects=True, vmem_limit_bytes=40 << 20
+            collective_id=0, has_side_effects=True, vmem_limit_bytes=56 << 20
         ),
-    )(raw, depth, interp[0], obs[0], counts)
-
-    mine = parent[lax.axis_index("member")]
-    everyone = lax.all_gather(forecast, "member", axis=0)
-    selected = jnp.arange(everyone.shape[0], dtype=jnp.int32) == mine
-    chosen = jnp.sum(jnp.where(selected[:, None, None], everyone, 0.0), axis=0)
-    misfits = lax.all_gather(misfit, "member", axis=0, tiled=True)
-    chosen_misfit = jnp.sum(jnp.where(selected, misfits, 0.0))
-    result = chosen.reshape(fields * levels, blocks, rows, 128).transpose(0, 2, 1, 3)
-    return result.reshape(state.shape), chosen_misfit.reshape(1)
+    )(raw, parent, depth, interp[0], obs[0], counts)
+    result = result.reshape(fields * levels, blocks, rows, 128).transpose(0, 2, 1, 3)
+    return result.reshape(state.shape), misfit
 
 
 def solution(mesh):
     return jax.shard_map(
-        functools.partial(per_device, mesh.shape["tile"]),
+        functools.partial(per_device, mesh.shape["tile"], mesh.shape["member"]),
         mesh=mesh,
         in_specs=(
             P(("parts", "member"), None, None, "tile", None),

time: 138 us -> 83 us (0.60)
  waiting for transfers between devices: 59.5 us -> 0 us
  Pallas kernels: 38.1 us -> 77.7 us
  blocking collectives: 12.5 us -> 0 us
  between operations: 14.7 us -> 2.96 us
  other arithmetic: 5.39 us -> 0 us
  local copies, waits for them, and re-layouts: 7.53 us -> 2.21 us
    all_gather x1 -> x0, waiting for transfers between devices: 59.5 us -> none  [per_device(): everyone = lax.all_gather(forecast, 'member', axis=0)]
    pallas_call x1, Pallas kernels: 38.1 us -> 77.7 us  [per_device(): pl.pallas_call(functools.partial(forecast_kernel, levels, tiles, members)...]
    unnamed x1 -> x0, blocking collectives: 12.5 us -> none
    reduce_sum x2 -> x0, other arithmetic: 4.74 us -> none  [the longest x1 3.5 us: per_device(): chosen = jnp.sum(jnp.where(selected[:, None, None], everyone, 0.0), axis=0)]
    unnamed x11 -> x1, local copies, waits for them, and re-layouts: 6.3 us -> 2.21 us
  transfers between devices with their start and end apart: 1 -> 0, of which waited for: 1 -> 0; matrix products, arithmetic and copies ran while one was open for 4% -> 0% of each run, Pallas kernels for 0% -> 0%
where the time goes in v2:
time: 83 us; the launch traced here: 82.8 us
  Pallas kernels  77.7 us (94%)
  between operations  2.96 us (4%)
  local copies, waits for them, and re-layouts  2.21 us (3%)
    pallas_call x1, Pallas kernels, per_device(): pl.pallas_call(functools.partial(forecast_kernel, levels, tiles, members)...  77.7 us
    unnamed x1, local copies, waits for them, and re-layouts  2.21 us

profile of v2, /device:TPU:0, one launch (start us, length us, event | category | flops | bytes accessed | tf_op | source)
XLA Modules:
  0.0 82.8 jit_solution(9664929280117210695)
XLA Ops:
  1.3 77.7 %shard_map.77 = (f32[1920,128]{1,0:T(8,128)}, f32[1]{0:T(128)}) custom-call(f32[1920,128]{1,0:T(8,128)} %bitcast.13, s32[4]{0:T(128)} %parent.1, f32[20]{0:T(128)} %depth.1, bf16[128,4096]{1,0:T(8,128)(2,1)} %bitcast.12, f32[2,128]{1,0:T(2,128)} %bitcast.15, s32[1]{0:T(128)S(6)} %copy.12.counts), custom_call_target="tpu_custom_call" | custom-call | tf_op jit(solution)/shard_map/pallas_call | solution.py:421
  78.9 2.2 %copy.13 = f32[1,3,20,4,1024]{4,3,2,1,0:T(4,128)} copy(f32[1,3,20,4,1024]{4,3,2,1,0:T(4,128)} %bitcast.14) | data formatting | bytes 1966080

commit v3 on v2

--- a/solution.py
+++ b/solution.py
@@ -9,6 +9,8 @@
 
 STEPS = 4
 GROUPS = 4
+PIECES = 2
+BATCH = 4
 U, H, V = 0, 1, 2
 SOURCE = {U: 0, V: 1, H: 2}
 MESH = pl.DeviceIdType.MESH
@@ -38,10 +40,11 @@
     levels, tiles, members,
     state, parent, depth, interp, obs, counts,
     out, misfit,
-    x, done, inbox, outbox, terms, member_terms,
+    x0, x1, x2, x3, done, inbox, outbox, terms, member_terms,
     send_sem, recv_sem, ship_send, ship_recv,
     term_send, term_recv, member_send, member_recv,
 ):
+    x = (x0, x1, x2, x3)
     tile = lax.axis_index("tile")
     right, left = lax.rem(tile + 1, tiles), lax.rem(tile + tiles - 1, tiles)
     barrier = pltpu.get_barrier_semaphore()
@@ -73,18 +76,18 @@
         def _(l):
             for f in (U, H, V):
                 for r in range(4):
-                    x[0, f, l, 2 + r] = state[raw(f, l, r), :]
+                    x0[f, l, 2 + r] = state[raw(f, l, r), :]
 
     def halo(group, t, side):
         low, high = span(group, t)
         lv = pl.ds(low, high - low)
         if side == 0:
-            pieces = ((x.at[t, pl.ds(0, 2), lv, pl.ds(4, 2)], x.at[t, pl.ds(0, 2), lv, pl.ds(0, 2)]),
-                      (x.at[t, V, lv, pl.ds(5, 1)], x.at[t, V, lv, pl.ds(1, 1)]))
+            pieces = ((x[t].at[pl.ds(0, 2), lv, pl.ds(4, 2)], x[t].at[pl.ds(0, 2), lv, pl.ds(0, 2)]),
+                      (x[t].at[V, lv, pl.ds(5, 1)], x[t].at[V, lv, pl.ds(1, 1)]))
             to = right
         else:
-            pieces = ((x.at[t, pl.ds(0, 2), lv, pl.ds(2, 2)], x.at[t, pl.ds(0, 2), lv, pl.ds(6, 2)]),
-                      (x.at[t, V, lv, pl.ds(2, 1)], x.at[t, V, lv, pl.ds(6, 1)]))
+            pieces = ((x[t].at[pl.ds(0, 2), lv, pl.ds(2, 2)], x[t].at[pl.ds(0, 2), lv, pl.ds(6, 2)]),
+                      (x[t].at[V, lv, pl.ds(2, 1)], x[t].at[V, lv, pl.ds(6, 1)]))
             to = left
         return [
             pltpu.make_async_remote_copy(
@@ -112,54 +115,78 @@
                 for copy in halo(group, t, side):
                     copy.wait_recv()
 
-    def cell(t, l, below, above):
-        u, h = x[t, U, l], x[t, H, l]
-        v = x[t, V, l, 1:7]
-        core = u[1:7]
-        u1 = (
-            (1.0 - time_step * (4.0 * viscosity + 2.0 * mixing)) * core
-            + (time_step * coriolis) * v
-            - (time_step * 0.5) * (h[2:8] - h[0:6])
-            + (time_step * viscosity) * ((u[2:8] + u[0:6]) + (west(core) + east(core)))
-            + (time_step * mixing) * (x[t, U, below, 1:7] + x[t, U, above, 1:7])
-        )
-        mid = v[1:5]
-        diffuse = (time_step * viscosity) * mid
-        slope = (time_step * 0.5) * h[2:6]
-        v1 = (
-            (1.0 - time_step * (4.0 * viscosity + 2.0 * mixing)) * mid
-            - (time_step * coriolis) * u[2:6]
-            + (time_step * viscosity) * (v[2:6] + v[0:4])
-            + (east(diffuse - slope) + west(diffuse + slope))
-            + (time_step * mixing) * (x[t, V, below, 2:6] + x[t, V, above, 2:6])
-        )
-        h1 = h[2:6] - (time_step * 0.5 * depth[l]) * (
-            (u1[2:6] - u1[0:4]) + (east(v1) - west(v1))
-        )
-        if t + 1 < STEPS:
-            x[t + 1, U, l, 2:6] = u1[1:5]
-            x[t + 1, V, l, 2:6] = v1
-            x[t + 1, H, l, 2:6] = h1
-        else:
-            done[U, l] = u1[1:5]
-            done[V, l] = v1
-            done[H, l] = h1
+    def cells(t, middle):
+        now = x[t]
+        us, vs = {}, {}
+        for place, (l, _, _) in enumerate(middle):
+            us[place], vs[place] = now[U, l], now[V, l, 1:7]
+        edge = len(middle)
+        (first, below, _), (final, _, above) = middle[0], middle[-1]
+        us[-1] = us[0] if below is first else now[U, below]
+        vs[-1] = vs[0] if below is first else now[V, below, 1:7]
+        us[edge] = us[edge - 1] if above is final else now[U, above]
+        vs[edge] = vs[edge - 1] if above is final else now[V, above, 1:7]
+        results = []
+        for place, (l, _, _) in enumerate(middle):
+            u, h, v = us[place], now[H, l], vs[place]
+            core = u[1:7]
+            u1 = (
+                (1.0 - time_step * (4.0 * viscosity + 2.0 * mixing)) * core
+                + (time_step * coriolis) * v
+                - (time_step * 0.5) * (h[2:8] - h[0:6])
+                + (time_step * viscosity) * ((u[2:8] + u[0:6]) + (west(core) + east(core)))
+                + (time_step * mixing) * (us[place - 1][1:7] + us[place + 1][1:7])
+            )
+            mid = v[1:5]
+            diffuse = (time_step * viscosity) * mid
+            slope = (time_step * 0.5) * h[2:6]
+            v1 = (
+                (1.0 - time_step * (4.0 * viscosity + 2.0 * mixing)) * mid
+                - (time_step * coriolis) * u[2:6]
+                + (time_step * viscosity) * (v[2:6] + v[0:4])
+                + (east(diffuse - slope) + west(diffuse + slope))
+                + (time_step * mixing) * (vs[place - 1][1:5] + vs[place + 1][1:5])
+            )
+            results.append((l, u1, v1, h[2:6]))
+        results = [
+            (l, u1[1:5], v1, h - (time_step * 0.5 * depth[l]) * (
+                (u1[2:6] - u1[0:4]) + (east(v1) - west(v1))
+            ))
+            for l, u1, v1, h in results
+        ]
+        for l, u1, v1, h1 in results:
+            if t + 1 < STEPS:
+                x[t + 1][U, l, 2:6] = u1
+                x[t + 1][V, l, 2:6] = v1
+                x[t + 1][H, l, 2:6] = h1
+            else:
+                done[U, l] = u1
+                done[V, l] = v1
+                done[H, l] = h1
 
     def advance(group, t):
         low, high = span(group, t + 1)
-        if low == 0:
-            cell(t, 0, 0, 1)
-            low = 1
-        last = high == levels
-        if last:
-            high = levels - 1
-
-        @pl.loop(low, high)
-        def _(l):
-            cell(t, l, l - 1, l + 1)
-
-        if last:
-            cell(t, levels - 1, levels - 2, levels - 1)
+
+        def neighbours(l):
+            if isinstance(l, int):
+                return l, max(l - 1, 0) if l else l, l if l == levels - 1 else l + 1
+            return l, l - 1, l + 1
+
+        count = high - low
+        whole = count // BATCH
+        odd = count - whole * BATCH
+        batches = [list(range(low + i * BATCH, low + (i + 1) * BATCH)) for i in range(whole)]
+        if odd:
+            batches.append(list(range(high - odd, high)))
+        inner = [i for i in range(whole) if batches[i][0] > 0 and batches[i][-1] < levels - 1]
+        for i, batch in enumerate(batches):
+            if i not in inner or len(inner) < 2:
+                cells(t, [neighbours(l) for l in batch])
+        if len(inner) >= 2:
+            @pl.loop(inner[0], inner[-1] + 1)
+            def _(i):
+                base = low + i * BATCH
+                cells(t, [neighbours(base + j) for j in range(BATCH)])
 
     row = lax.broadcasted_iota(jnp.int32, (8, 128), 0)
     live = lax.broadcasted_iota(jnp.int32, (1, 128), 1) < counts[0]
@@ -168,7 +195,7 @@
         pieces = []
         for r in range(4):
             if t < STEPS:
-                u, v = x[t, U, 0, 2 + r], x[t, V, 0, 2 + r]
+                u, v = x[t][U, 0, 2 + r], x[t][V, 0, 2 + r]
             else:
                 u, v = done[U, 0, r], done[V, 0, r]
             for block in range(8):
@@ -198,7 +225,7 @@
                 for block in range(8):
                     at = (r * 8 + block) * 128
                     total = jnp.where(row == block, back[8 * k:8 * k + 8, at:at + 128], total)
-                x[t, f, 0, 2 + r] += (time_step * nudge_gain) * total
+                x[t][f, 0, 2 + r] += (time_step * nudge_gain) * total
 
     half = members // 2
     place = (me, members - 1 - me)
@@ -210,38 +237,46 @@
     def is_value(value, number):
         return jnp.broadcast_to((jnp.full((8, 128), value, jnp.int32) == number)[None], (4, 8, 128))
 
-    def ship(way, source, slot, group):
-        low, high = span(group, STEPS)
+    def pieces_of(group):
+        return range(group * PIECES, (group + 1) * PIECES)
+
+    def bounds(piece):
+        low, high = span(piece // PIECES, STEPS)
+        count, part = high - low, PIECES - 1 - piece % PIECES
+        return low + count * part // PIECES, low + count * (part + 1) // PIECES
+
+    def ship(way, source, slot, piece):
+        low, high = bounds(piece)
         lv = pl.ds(low, high - low)
         return pltpu.make_async_remote_copy(
             src_ref=source.at[:, lv], dst_ref=inbox.at[way, slot, :, lv],
-            send_sem=ship_send.at[way, slot, group], recv_sem=ship_recv.at[way, slot, group],
+            send_sem=ship_send.at[way, slot, piece], recv_sem=ship_recv.at[way, slot, piece],
             device_id={"member": following[way]}, device_id_type=MESH,
         )
 
-    def ship_own(group):
+    def ship_own(piece):
         for way in (0, 1):
             @pl.when(place[way] < half)
             def _():
-                ship(way, done, place[way], group).start()
-
-    def relay(group):
+                ship(way, done, place[way], piece).start()
+
+    def relay(piece):
         for way in (0, 1):
             @pl.when(place[way] < half)
             def _():
                 @pl.loop(0, place[way])
                 def _(slot):
-                    ship(way, done, slot, group).wait_recv()
-                    ship(way, inbox.at[way, slot], slot, group).start()
-
-    def take(group):
-        low, high = span(group, STEPS)
+                    ship(way, done, slot, piece).wait_recv()
+                    ship(way, inbox.at[way, slot], slot, piece).start()
+
+    def take(piece):
+        low, high = bounds(piece)
         for way in (0, 1):
             @pl.when(place[way] == half)
             def _():
                 @pl.loop(0, half)
                 def _(slot):
-                    ship(way, done, slot, group).wait_recv()
+                    ship(way, done, slot, piece).wait_recv()
 
                 @pl.loop(half + 1, members)
                 def _(receiver):
@@ -257,13 +292,13 @@
                                 value = jnp.where(masks[other], inbox[way, other, f, l], value)
                             outbox[way, slot, f, l] = value
 
-                    ship(way, outbox.at[way, slot], slot, group).start()
+                    ship(way, outbox.at[way, slot], slot, piece).start()
 
             @pl.when(place[way] > half)
             def _():
                 @pl.loop(place[way], members)
                 def _(receiver):
-                    ship(way, done, receiver - half - 1, group).wait_recv()
+                    ship(way, done, receiver - half - 1, piece).wait_recv()
 
                 @pl.loop(place[way] + 1, members)
                 def _(receiver):
@@ -277,10 +312,10 @@
                                 own, done[f, l], inbox[way, slot, f, l]
                             )
 
-                    ship(way, outbox.at[way, slot], slot, group).start()
-
-    def finish(group):
-        low, high = span(group, STEPS)
+                    ship(way, outbox.at[way, slot], slot, piece).start()
+
+    def finish(piece):
+        low, high = bounds(piece)
         masks = []
         for way in (0, 1):
             wanted = parent_place(way, place[way])
@@ -300,19 +335,19 @@
                 for r in range(4):
                     out[raw(f, l, r), :] = value[r]
 
-    def shipped(group):
+    def shipped(piece):
         for way in (0, 1):
             @pl.when(place[way] < half)
             def _():
                 @pl.loop(0, place[way] + 1)
                 def _(slot):
-                    ship(way, done, slot, group).wait_send()
+                    ship(way, done, slot, piece).wait_send()
 
             @pl.when(place[way] >= half)
             def _():
                 @pl.loop(place[way] + 1, members)
                 def _(receiver):
-                    ship(way, done, receiver - half - 1, group).wait_send()
+                    ship(way, done, receiver - half - 1, piece).wait_send()
 
     for side, rows in ((0, 0), (1, 6)):
         @pl.when(jnp.logical_not(receives[side]))
@@ -321,7 +356,7 @@
             def _(l):
                 for t in range(STEPS):
                     for f in (U, H, V):
-                        x[t, f, l, rows:rows + 2] = jnp.zeros((2, 8, 128), jnp.float32)
+                        x[t][f, l, rows:rows + 2] = jnp.zeros((2, 8, 128), jnp.float32)
 
     load(0)
     pl.semaphore_wait(barrier, tiles + members - 2)
@@ -343,10 +378,11 @@
                         nudge(t + 1)
                     send(group, t + 1)
                 else:
-                    ship_own(group)
-        ready = stage - STEPS - 1
-        if ready >= 0:
-            relay(ready)
+                    for piece in pieces_of(group):
+                        ship_own(piece)
+        if stage >= STEPS:
+            for piece in pieces_of(stage - STEPS):
+                relay(piece)
 
     part_u, part_v = residual(STEPS)
     terms[pl.ds(tile, 1)] = jnp.broadcast_to(
@@ -368,8 +404,9 @@
         ))
     for copy, _ in copies:
         copy.start()
-    for group in range(last - STEPS - 1, GROUPS):
-        relay(group)
+    for group in range(last - STEPS, GROUPS):
+        for piece in pieces_of(group):
+            relay(piece)
     for copy, arrival in copies:
         copy.wait_send()
         arrival.wait_recv()
@@ -387,9 +424,9 @@
             ))
     for copy in copies[::2]:
         copy.start()
-    for group in range(GROUPS):
-        take(group)
-        finish(group)
+    for piece in range(GROUPS * PIECES):
+        take(piece)
+        finish(piece)
     for copy, arrival in zip(copies[::2], copies[1::2]):
         copy.wait_send()
         arrival.wait_recv()
@@ -405,8 +442,8 @@
                 def _():
                     for copy in halo(group, t, side):
                         copy.wait_send()
-    for group in range(GROUPS):
-        shipped(group)
+    for piece in range(GROUPS * PIECES):
+        shipped(piece)
 
 
 def per_device(tiles, members, state, parent, depth, interp, obs, counts):
@@ -427,14 +464,14 @@
         in_specs=[vmem, smem, smem, vmem, vmem, smem],
         out_specs=(vmem, smem),
         scratch_shapes=[
-            pltpu.VMEM((STEPS, fields, levels, rows + 4, blocks, 128), jnp.float32),
+            *[pltpu.VMEM((fields, levels, rows + 4, blocks, 128), jnp.float32)] * STEPS,
             pltpu.VMEM(whole, jnp.float32),
             pltpu.VMEM((2, half) + whole, jnp.float32),
             pltpu.VMEM((2, max(half - 1, 1)) + whole, jnp.float32),
             pltpu.VMEM((tiles, 8, 128), jnp.float32),
             pltpu.VMEM((members, 8, 128), jnp.float32),
             dma((STEPS, GROUPS, 2, 2)), dma((STEPS, GROUPS, 2, 2)),
-            dma((2, half, GROUPS)), dma((2, half, GROUPS)),
+            dma((2, half, GROUPS * PIECES)), dma((2, half, GROUPS * PIECES)),
             dma((tiles,)), dma((tiles,)),
             dma((members,)), dma((members,)),
         ],

time: 83 us -> 78.1 us (0.941)
  Pallas kernels: 77.7 us -> 72 us
    pallas_call x1, Pallas kernels: 77.7 us -> 72 us  [per_device(): pl.pallas_call(functools.partial(forecast_kernel, levels, tiles, members)...]
where the time goes in v3:
time: 78.1 us; the launch traced here: 77.1 us
  Pallas kernels  72 us (92%)
  between operations  2.96 us (4%)
  local copies, waits for them, and re-layouts  2.21 us (3%)
    pallas_call x1, Pallas kernels, per_device(): pl.pallas_call(functools.partial(forecast_kernel, levels, tiles, members)...  72 us
    unnamed x1, local copies, waits for them, and re-layouts  2.21 us

profile of v3, /device:TPU:0, one launch (start us, length us, event | category | flops | bytes accessed | tf_op | source)
XLA Modules:
  0.0 77.1 jit_solution(1601283836206462244)
XLA Ops:
  1.3 72.0 %shard_map.77 = (f32[1920,128]{1,0:T(8,128)}, f32[1]{0:T(128)}) custom-call(f32[1920,128]{1,0:T(8,128)} %bitcast.13, s32[4]{0:T(128)} %parent.1, f32[20]{0:T(128)} %depth.1, bf16[128,4096]{1,0:T(8,128)(2,1)} %bitcast.12, f32[2,128]{1,0:T(2,128)} %bitcast.15, s32[1]{0:T(128)S(6)} %copy.12.counts), custom_call_target="tpu_custom_call" | custom-call | tf_op jit(solution)/shard_map/pallas_call | solution.py:458
  73.2 2.2 %copy.13 = f32[1,3,20,4,1024]{4,3,2,1,0:T(4,128)} copy(f32[1,3,20,4,1024]{4,3,2,1,0:T(4,128)} %bitcast.14) | data formatting | bytes 1966080
